TPU v7x, 32 devices: a whole 2x2x4 slice. The times are simulated.
32 devices in a mesh: row: 4 (over z), col: 8 (over y, x, core).
Axes of the slice: x: 2, y: 2, z: 4, core: 2. Of those that a mesh axis runs over, the one named last changes fastest.
Arguments:
- field_in: float32 [16, 32, 64, 4], P(None, 'row', 'col'), may hold values from -6 to 6
- conv_weight: float32 [3, 3, 4, 256], replicated, may hold values from -1 to 1
- conv_bias: float32 [256], replicated, may hold values from -3 to 3
- first_gain: float32 [256], replicated, may hold values from 0.5 to 1.5
- first_shift: float32 [256], replicated, may hold values from -3 to 3
- query_weight: float32 [256, 256], replicated, may hold values from -0.375 to 0.375
- key_weight: float32 [256, 256], replicated, may hold values from -0.375 to 0.375
- value_weight: float32 [256, 256], replicated, may hold values from -0.375 to 0.375
- output_weight: float32 [256, 256], replicated, may hold values from -1 to 1
- second_gain: float32 [256], replicated, may hold values from 0.5 to 1.5
- second_shift: float32 [256], replicated, may hold values from -3 to 3
- hidden_weight: float32 [256, 512], replicated, may hold values from -0.375 to 0.375
- hidden_bias: float32 [512], replicated, may hold values from -3 to 3
- return_weight: float32 [512, 256], replicated, may hold values from -0.25 to 0.25
- return_bias: float32 [256], replicated, may hold values from -3 to 3
- decode_query: float32 [128, 256], replicated, may hold values from -0.5 to 0.5
- decode_key: float32 [256, 256], replicated, may hold values from -0.375 to 0.375
- decode_value: float32 [256, 256], replicated, may hold values from -0.375 to 0.375
- decode_output: float32 [256, 256], replicated, may hold values from -1 to 1
- propagate_up: float32 [256, 512], replicated, may hold values from -0.375 to 0.375
- propagate_bias: float32 [512], replicated, may hold values from -3 to 3
- propagate_down: float32 [512, 256], replicated, may hold values from -0.25 to 0.25
- propagate_shift: float32 [256], replicated, may hold values from -3 to 3
- cotangent: float32 [16, 32, 64, 256], P(None, 'row', 'col'), may hold values from -6 to 6
- grid_sizes: int32 [16, 2], replicated, may hold values from 16 to 64, as said below
Outputs:
- result_field: float32 [16, 32, 64, 256], P(None, 'row', 'col')
- field_grad: float32 [16, 32, 64, 4], P(None, 'row', 'col')
- conv_weight_grad: float32 [3, 3, 4, 256], replicated
- conv_bias_grad: float32 [256], replicated
- first_gain_grad: float32 [256], replicated
- first_shift_grad: float32 [256], replicated
- query_weight_grad: float32 [256, 256], replicated
- key_weight_grad: float32 [256, 256], replicated
- value_weight_grad: float32 [256, 256], replicated
- output_weight_grad: float32 [256, 256], replicated
- second_gain_grad: float32 [256], replicated
- second_shift_grad: float32 [256], replicated
- hidden_weight_grad: float32 [256, 512], replicated
- hidden_bias_grad: float32 [512], replicated
- return_weight_grad: float32 [512, 256], replicated
- return_bias_grad: float32 [256], replicated
- decode_query_grad: float32 [128, 256], replicated
- decode_key_grad: float32 [256, 256], replicated
- decode_value_grad: float32 [256, 256], replicated
- decode_output_grad: float32 [256, 256], replicated
- propagate_up_grad: float32 [256, 512], replicated
- propagate_bias_grad: float32 [512], replicated
- propagate_down_grad: float32 [512, 256], replicated
- propagate_shift_grad: float32 [256], replicated
Inputs may be any that keep to these rules, and one draw needn't show every extreme that they name: `grid_sizes`: each item's valid rows are at most 32 and valid columns at most 64; in every draw one item covers the whole padded grid.
All inputs are finite; a program needn't handle non-finite values.
Results may differ from a plain program's by a relative error of at most 0.0003.
Values sent between devices are 32-bit elements; how exact they have to be, the bound alone decides.
A program may use at most 192 MiB of HBM per device.

v0:
```python
import math

import jax
import jax.numpy as jnp
from jax import lax
from jax.sharding import PartitionSpec as P

HEADS = 8
HEAD = 32
FOUR = 128
MICRO = 4


highest = lax.Precision.HIGHEST


def padded_2(x, sides, width):
    for axis, dim in sides:
        size, length = (lax.axis_size(axis), x.shape[dim])
        up = [(i, (i + 1) % size) for i in range(size - 1)]
        down = [(j, i) for i, j in up]
        last = lax.slice_in_dim(x, length - width, length, axis=dim)
        leading = lax.slice_in_dim(x, 0, width, axis=dim)
        before = lax.ppermute(last, axis, up)
        after = lax.ppermute(leading, axis, down)
        x = jnp.concatenate([before, x, after], axis=dim)
    return x


def matmul(left, right):
    return jnp.matmul(left, right, precision=highest)


def smooth(values):
    return jax.nn.gelu(values, approximate=True)


def layer_norm(values, norm_gain, norm_shift):
    average = jnp.mean(values, axis=-1, keepdims=True)
    center = values - average
    spread = jnp.mean(center * center, axis=-1, keepdims=True)
    return center * lax.rsqrt(spread + 1e-05) * norm_gain + norm_shift


def geometry(row_index, col_index, grid_sizes):
    size_rows = grid_sizes[:, 0]
    size_cols = grid_sizes[:, 1]
    within = (row_index[None, :, None] < size_rows[:, None, None]) & (
        col_index[None, None, :] < size_cols[:, None, None]
    )
    inside = within.astype(jnp.float32)
    coord_x = (row_index.astype(jnp.float32)[None, :, None] + 0.5) / size_rows.astype(jnp.float32)[
        :, None, None
    ] + 0.0 * inside
    coord_y = (col_index.astype(jnp.float32)[None, None, :] + 0.5) / size_cols.astype(jnp.float32)[
        :, None, None
    ] + 0.0 * inside
    points = (size_rows * size_cols).astype(jnp.float32)
    return (inside, coord_x, coord_y, points)


def features(coord_x, coord_y):
    angles = math.pi * (jnp.arange(FOUR // 4).astype(jnp.float32) + 1.0)
    along_x = coord_x[..., None] * angles
    along_y = coord_y[..., None] * angles
    return jnp.concatenate(
        [jnp.sin(along_x), jnp.cos(along_x), jnp.sin(along_y), jnp.cos(along_y)], axis=-1
    )


def rotate(vectors, coord_x, coord_y):
    quarter = HEAD // 4
    angles = 2.0 * math.pi * (jnp.arange(quarter).astype(jnp.float32) + 1.0)
    turn_x = coord_x[..., None, None] * angles
    turn_y = coord_y[..., None, None] * angles
    cosine_x, sine_x = (jnp.cos(turn_x), jnp.sin(turn_x))
    cosine_y, sine_y = (jnp.cos(turn_y), jnp.sin(turn_y))
    part_one = vectors[..., :quarter]
    part_two = vectors[..., quarter : 2 * quarter]
    part_three = vectors[..., 2 * quarter : 3 * quarter]
    part_four = vectors[..., 3 * quarter :]
    return jnp.concatenate(
        [
            part_one * cosine_x - part_two * sine_x,
            part_one * sine_x + part_two * cosine_x,
            part_three * cosine_y - part_four * sine_y,
            part_three * sine_y + part_four * cosine_y,
        ],
        axis=-1,
    )


def split_heads(values):
    return values.reshape(values.shape[:-1] + (HEADS, HEAD))


def conv_embed(padded, weight_in, bias_in):
    tile_rows = padded.shape[1] - 2
    tile_cols = padded.shape[2] - 2
    total = jnp.zeros(padded.shape[:1] + (tile_rows, tile_cols, weight_in.shape[-1]), jnp.float32)
    for shift_row in range(3):
        for shift_col in range(3):
            window = padded[
                :, shift_row : shift_row + tile_rows, shift_col : shift_col + tile_cols, :
            ]
            total = total + jnp.einsum(
                "brci,io->brco", window, weight_in[shift_row, shift_col], precision=highest
            )
    return total + bias_in


def conv_transpose(grad_padded, weight_in):
    tile_rows = grad_padded.shape[1] - 2
    tile_cols = grad_padded.shape[2] - 2
    total = jnp.zeros(
        grad_padded.shape[:1] + (tile_rows, tile_cols, weight_in.shape[2]), jnp.float32
    )
    for shift_row in range(3):
        for shift_col in range(3):
            window = grad_padded[
                :,
                2 - shift_row : 2 - shift_row + tile_rows,
                2 - shift_col : 2 - shift_col + tile_cols,
                :,
            ]
            total = total + jnp.einsum(
                "brco,io->brci", window, weight_in[shift_row, shift_col], precision=highest
            )
    return total


def project(params, hidden0, coord_x, coord_y):
    first_gain, first_shift, query_weight, key_weight, value_weight = params
    normed = layer_norm(hidden0, first_gain, first_shift)
    query_heads = rotate(split_heads(matmul(normed, query_weight)), coord_x, coord_y)
    key_heads = rotate(split_heads(matmul(normed, key_weight)), coord_x, coord_y)
    value_heads = split_heads(matmul(normed, value_weight))
    return (query_heads, key_heads, value_heads)


def summary(key_heads, value_heads, weight):
    return jnp.einsum(
        "brchd,brche->bhde", key_heads * weight[..., None, None], value_heads, precision=highest
    )


def encoder_rest(params, hidden0, query_heads, kv_summary):
    (
        output_weight,
        second_gain,
        second_shift,
        hidden_weight,
        hidden_bias,
        return_weight,
        return_bias,
    ) = params
    mixed = jnp.einsum("brchd,bhde->brche", query_heads, kv_summary, precision=highest).reshape(
        hidden0.shape
    )
    hidden1 = hidden0 + matmul(mixed, output_weight)
    normed = layer_norm(hidden1, second_gain, second_shift)
    return (
        hidden1
        + matmul(smooth(matmul(normed, hidden_weight) + hidden_bias), return_weight)
        + return_bias
    )


def decode_summary(params, hidden2, weight):
    decode_key, decode_value = params
    return summary(
        split_heads(matmul(hidden2, decode_key)), split_heads(matmul(hidden2, decode_value)), weight
    )


def decode_out(params, fourier, dec_summary, inside):
    decode_query, decode_output, propagate_up, propagate_bias, propagate_down, propagate_shift = (
        params
    )
    query_heads = split_heads(matmul(fourier, decode_query))
    mixed = jnp.einsum("brchd,bhde->brche", query_heads, dec_summary, precision=highest)
    latent = matmul(mixed.reshape(mixed.shape[:-2] + (HEADS * HEAD,)), decode_output)
    result = (
        latent
        + matmul(smooth(matmul(latent, propagate_up) + propagate_bias), propagate_down)
        + propagate_shift
    )
    return result * inside[..., None]


def accumulate(running, fresh):
    if running is None:
        return fresh
    return jax.tree.map(lambda left, right: left + right, running, fresh)


def body(
    field_in,
    conv_weight,
    conv_bias,
    first_gain,
    first_shift,
    query_weight,
    key_weight,
    value_weight,
    output_weight,
    second_gain,
    second_shift,
    hidden_weight,
    hidden_bias,
    return_weight,
    return_bias,
    decode_query,
    decode_key,
    decode_value,
    decode_output,
    propagate_up,
    propagate_bias,
    propagate_down,
    propagate_shift,
    cotangent,
    grid_sizes,
):
    tile_rows = field_in.shape[1]
    tile_cols = field_in.shape[2]
    per_items = field_in.shape[0] // MICRO
    row_index = lax.axis_index("row") * tile_rows + jnp.arange(tile_rows, dtype=jnp.int32)
    col_index = lax.axis_index("col") * tile_cols + jnp.arange(tile_cols, dtype=jnp.int32)
    front_params = (first_gain, first_shift, query_weight, key_weight, value_weight)
    rest_params = (
        output_weight,
        second_gain,
        second_shift,
        hidden_weight,
        hidden_bias,
        return_weight,
        return_bias,
    )
    pair_params = (decode_key, decode_value)
    out_params = (
        decode_query,
        decode_output,
        propagate_up,
        propagate_bias,
        propagate_down,
        propagate_shift,
    )
    decoder_total = None
    encoder_total = None
    results = []
    field_grads = []
    for micro in range(MICRO):
        first_item = micro * per_items
        field_part = field_in[first_item : first_item + per_items]
        cot_part = cotangent[first_item : first_item + per_items]
        sizes_part = grid_sizes[first_item : first_item + per_items]
        inside, coord_x, coord_y, points = geometry(row_index, col_index, sizes_part)
        fourier = features(coord_x, coord_y)
        weight = inside / points[:, None, None]
        padded = padded_2(field_part * inside[..., None], (("row", 1), ("col", 2)), 1)
        hidden0 = conv_embed(padded, conv_weight, conv_bias)
        query_heads, key_heads, value_heads = project(front_params, hidden0, coord_x, coord_y)
        kv_summary = lax.psum(summary(key_heads, value_heads, weight), ("row", "col"))
        hidden2 = encoder_rest(rest_params, hidden0, query_heads, kv_summary)
        dec_summary = lax.psum(decode_summary(pair_params, hidden2, weight), ("row", "col"))

        def decode_local(params, summary_in):
            return decode_out(params, fourier, summary_in, inside)

        result, out_back = jax.vjp(decode_local, out_params, dec_summary)
        out_grads, dec_part = out_back(cot_part)
        dec_grad = lax.psum(dec_part, ("row", "col"))

        def pair_local(params, hidden_in):
            return decode_summary(params, hidden_in, weight)

        pair_back = jax.vjp(pair_local, pair_params, hidden2)[1]
        pair_grads, hidden2_grad = pair_back(dec_grad)
        decoder_total = accumulate(
            decoder_total,
            (
                out_grads[0],
                pair_grads[0],
                pair_grads[1],
                out_grads[1],
                out_grads[2],
                out_grads[3],
                out_grads[4],
                out_grads[5],
            ),
        )
        rest_back = jax.vjp(encoder_rest, rest_params, hidden0, query_heads, kv_summary)[1]
        rest_grads, hidden0_part, query_grad, kv_part = rest_back(hidden2_grad)
        kv_grad = lax.psum(kv_part, ("row", "col"))

        def summary_local(key_in, value_in):
            return summary(key_in, value_in, weight)

        key_grad, value_grad = jax.vjp(summary_local, key_heads, value_heads)[1](kv_grad)

        def project_local(params, hidden_in):
            return project(params, hidden_in, coord_x, coord_y)

        front_grads, hidden0_more = jax.vjp(project_local, front_params, hidden0)[1](
            (query_grad, key_grad, value_grad)
        )
        hidden0_grad = hidden0_part + hidden0_more

        def conv_local(weight_in, bias_in):
            return conv_embed(padded, weight_in, bias_in)

        conv_grads = jax.vjp(conv_local, conv_weight, conv_bias)[1](hidden0_grad)
        grad_padded = padded_2(hidden0_grad, (("row", 1), ("col", 2)), 1)
        field_grad = conv_transpose(grad_padded, conv_weight) * inside[..., None]
        encoder_total = accumulate(
            encoder_total,
            (
                conv_grads[0],
                conv_grads[1],
                front_grads[0],
                front_grads[1],
                front_grads[2],
                front_grads[3],
                front_grads[4],
                rest_grads[0],
                rest_grads[1],
                rest_grads[2],
                rest_grads[3],
                rest_grads[4],
                rest_grads[5],
                rest_grads[6],
            ),
        )
        results.append(result)
        field_grads.append(field_grad)
    totals = lax.psum(tuple(encoder_total) + tuple(decoder_total), ("row", "col"))
    result_field = jnp.concatenate(results, axis=0)
    field_grad_all = jnp.concatenate(field_grads, axis=0)
    return (
        result_field,
        field_grad_all,
        totals[0],
        totals[1],
        totals[2],
        totals[3],
        totals[4],
        totals[5],
        totals[6],
        totals[7],
        totals[8],
        totals[9],
        totals[10],
        totals[11],
        totals[12],
        totals[13],
        totals[14],
        totals[15],
        totals[16],
        totals[17],
        totals[18],
        totals[19],
        totals[20],
        totals[21],
    )


def solution(mesh):
    placed = (
        P(None, "row", "col", None),
        P(),
        P(),
        P(),
        P(),
        P(),
        P(),
        P(),
        P(),
        P(),
        P(),
        P(),
        P(),
        P(),
        P(),
        P(),
        P(),
        P(),
        P(),
        P(),
        P(),
        P(),
        P(),
        P(None, "row", "col", None),
        P(),
    )
    return jax.shard_map(
        body,
        mesh=mesh,
        in_specs=placed,
        out_specs=(
            P(None, "row", "col", None),
            P(None, "row", "col", None),
            P(),
            P(),
            P(),
            P(),
            P(),
            P(),
            P(),
            P(),
            P(),
            P(),
            P(),
            P(),
            P(),
            P(),
            P(),
            P(),
            P(),
            P(),
            P(),
            P(),
            P(),
            P(),
        ),
        check_vma=False,
    )
```

profile of v0, /device:TPU:0, one launch (start us, length us, event | category | flops | bytes accessed | tf_op | source)
XLA Modules:
  0.0 1400.2 jit_solution(7017255666170250645)
XLA Ops:
  10.7 4.9 collective-permute-start
  17.9 4.5 collective-permute-start.8
  24.8 4.5 collective-permute-start.4
  42.3 3.1 multiply_cosine_fusion.15
  47.4 4.5 collective-permute-start.12
  53.6 4.1 collective-permute-done.13
  60.4 4.8 collective-permute-start.6
  66.9 3.6 collective-permute-start.2
  73.7 3.0 collective-permute-start.10
  127.5 3.3 fusion.903
  140.4 3.6 multiply_subtract_fusion
  182.5 3.9 pad_maximum_fusion.2
  188.3 131.9 %all-reduce.88.cloned.1.call-done = (f32[4,8,32,32]{3,2,1,0:T(8,128)}, f32[4,8,32,32]{3,2,1,0:T(8,128)}, f32[4,8,32,32]{3,2,1,0:T(8,128)}, f32[4,8,32,32]{3,2,1,0:T(8,128)}) async-done(((f32[4,8,32,32]{3,2,1,0:T(8,128)}, f32[4,8,32,32]{3,2,1,0:T(8,128)}, f32[4,8,32,32]{3,2,1,0:T(8,128)}, f32[4,8,32,32]{3,2,1,0:T(8,128)}), (f32[4,8,32,32]{3,2,1,0:T(8,128)}, f32[4,8,32,32]{3,2,1,0:T(8,128)}, ...) | async-done | bytes 524304 | tf_op jit(solution)/shard_map/psum | solution.py:263
  369.1 4.6 convolution_bitcast_fusion.40
  373.7 3.6 convolution_bitcast_fusion.42
  377.3 3.6 convolution_bitcast_fusion.44
  381.0 3.5 convolution_bitcast_fusion.46
  392.2 126.0 %all-reduce.86.cloned.1.call-done = (f32[4,8,32,32]{3,2,1,0:T(8,128)}, f32[4,8,32,32]{3,2,1,0:T(8,128)}, f32[4,8,32,32]{3,2,1,0:T(8,128)}, f32[4,8,32,32]{3,2,1,0:T(8,128)}) async-done(((f32[4,8,32,32]{3,2,1,0:T(8,128)}, f32[4,8,32,32]{3,2,1,0:T(8,128)}, f32[4,8,32,32]{3,2,1,0:T(8,128)}, f32[4,8,32,32]{3,2,1,0:T(8,128)}), (f32[4,8,32,32]{3,2,1,0:T(8,128)}, f32[4,8,32,32]{3,2,1,0:T(8,128)}, ...) | async-done | bytes 524304 | tf_op jit(solution)/shard_map/psum | solution.py:265
  537.7 4.3 convolution_bitcast_fusion.33
  565.0 4.3 convolution_bitcast_fusion.35
  590.6 4.3 convolution_bitcast_fusion.37
  611.2 4.3 convolution_bitcast_fusion.39
  615.4 3.4 convolution_bitcast_fusion.3
  637.2 3.7 fusion.27
  648.0 130.6 %all-reduce.84.cloned.1.call-done = (f32[4,8,32,32]{3,2,1,0:T(8,128)}, f32[4,8,32,32]{3,2,1,0:T(8,128)}, f32[4,8,32,32]{3,2,1,0:T(8,128)}, f32[4,8,32,32]{3,2,1,0:T(8,128)}) async-done(((f32[4,8,32,32]{3,2,1,0:T(8,128)}, f32[4,8,32,32]{3,2,1,0:T(8,128)}, f32[4,8,32,32]{3,2,1,0:T(8,128)}, f32[4,8,32,32]{3,2,1,0:T(8,128)}), (f32[4,8,32,32]{3,2,1,0:T(8,128)}, f32[4,8,32,32]{3,2,1,0:T(8,128)}, ...) | async-done | bytes 524304 | tf_op jit(solution)/shard_map/psum | solution.py:272
  778.6 3.6 fusion.13
  782.2 3.0 convolution_bitcast_fusion.8
  785.2 3.0 fusion.9
  788.2 3.0 convolution_bitcast_fusion.13
  791.2 2.9 fusion.5
  897.8 4.0 convolution_bitcast_fusion.32
  907.8 4.0 convolution_bitcast_fusion.38
  915.2 4.2 convolution_bitcast_fusion.36
  919.4 3.6 convolution_bitcast_fusion.14
  963.8 128.6 %all-reduce.82.cloned.1.call-done = (f32[4,8,32,32]{3,2,1,0:T(8,128)}, f32[4,8,32,32]{3,2,1,0:T(8,128)}, f32[4,8,32,32]{3,2,1,0:T(8,128)}, f32[4,8,32,32]{3,2,1,0:T(8,128)}) async-done(((f32[4,8,32,32]{3,2,1,0:T(8,128)}, f32[4,8,32,32]{3,2,1,0:T(8,128)}, f32[4,8,32,32]{3,2,1,0:T(8,128)}, f32[4,8,32,32]{3,2,1,0:T(8,128)}), (f32[4,8,32,32]{3,2,1,0:T(8,128)}, f32[4,8,32,32]{3,2,1,0:T(8,128)}, ...) | async-done | bytes 524304 | tf_op jit(solution)/shard_map/psum | solution.py:294
  1092.4 3.3 fusion.15
  1101.7 3.0 fusion.7
  1139.0 3.6 multiply_add_fusion.7
  1213.4 3.2 collective-permute-start.24
  1217.9 4.5 collective-permute-start.16
  1223.8 4.9 collective-permute-start.28
  1240.7 40.6 %all-reduce.68 = (f32[3,3,4,256]{3,2,1,0:T(4,128)}, f32[256]{0:T(256)}, f32[256]{0:T(256)}, f32[256]{0:T(256)}, f32[256]{0:T(256)}, /*index=5*/f32[256]{0:T(256)...) all-reduce(f32[3,3,4,256]{3,2,1,0:T(4,128)S(1)} %add_add_fusion.16,, ...), channel_id=1, replica_groups=mesh['row'=4,'col'=8] {'row','col'}, use_global_device_ids=true, to_apply=%region_48.0 | all-reduce | flops 12032 | bytes 96256 | tf_op jit(solution)/shard_map/psum | solution.py:336
  1294.7 3.2 collective-permute-done.29
  1301.0 3.0 collective-permute-start.23
  1312.3 4.5 collective-permute-start.27
  1320.1 4.3 collective-permute-start.19
  1331.9 3.9 collective-permute-start.31
  1374.5 6.8 all-reduce.80.cloned.1.call-done
  (1643 shorter events, 655.8 us)
Async XLA Ops:
  7.2 318.3 %copy-start = (f32[256,512]{1,0:T(8,128)S(1)}, f32[256,512]{1,0:T(8,128)}, u32[]{:S(2)}) copy-start(f32[256,512]{1,0:T(8,128)} %param.36) | copy-start | bytes 1572868
  7.2 313.0 %all-reduce.88.cloned.1.call-start = ((), (), s32[]{:S(2)}) async-start(), calls=%async_computation.4 | async-start | bytes 4194304 | tf_op jit(solution)/shard_map/psum | solution.py:263
  10.7 67.4 %copy-start.90 = (f32[4,8,8,4]{2,3,1,0:T(4,128)}, f32[4,8,8,4]{2,3,1,0:T(4,128)S(1)}, u32[]{:S(2)}) copy-start(f32[4,8,8,4]{2,3,1,0:T(4,128)S(1)} %broadcast_multiply_fusion.3) | copy-start | bytes 12292
  10.7 35.4 %collective-permute-start = (f32[4,1,8,4]{2,3,1,0:T(4,128)S(1)}, f32[4,1,8,4]{2,3,1,0:T(4,128)S(1)}, u32[]{:S(2)}, u32[]{:S(2)}) collective-permute-start(f32[4,1,8,4]{2,3,1,0:T(4,128)S(1)} %get-tuple-element.334), channel_id=1, source_target_pairs={{0,8},{8,16},{16,24},{1,9},{9,17},{17,25},{2,10},{10,18},{18,26},{... | collective-permute-start | bytes 1544 | tf_op jit(solution)/shard_map/ppermute | solution.py:24
  15.6 31.8 %collective-permute-start.1 = (f32[4,1,8,4]{2,3,1,0:T(4,128)S(1)}, f32[4,1,8,4]{2,3,1,0:T(4,128)S(1)}, u32[]{:S(2)}, u32[]{:S(2)}) collective-permute-start(f32[4,1,8,4]{2,3,1,0:T(4,128)S(1)} %get-tuple-element.335), channel_id=1, source_target_pairs={{8,0},{16,8},{24,16},{9,1},{17,9},{25,17},{10,2},{18,10},{26,18},{... | collective-permute-start | bytes 1544 | tf_op jit(solution)/shard_map/ppermute | solution.py:25
  17.9 64.0 %copy-start.92 = (f32[4,8,8,4]{2,3,1,0:T(4,128)}, f32[4,8,8,4]{2,3,1,0:T(4,128)S(1)}, u32[]{:S(2)}) copy-start(f32[4,8,8,4]{2,3,1,0:T(4,128)S(1)} %broadcast_multiply_fusion.1) | copy-start | bytes 12292
  17.9 53.1 %collective-permute-start.8 = (f32[4,1,8,4]{2,3,1,0:T(4,128)S(1)}, f32[4,1,8,4]{2,3,1,0:T(4,128)S(1)}, u32[]{:S(2)}, u32[]{:S(2)}) collective-permute-start(f32[4,1,8,4]{2,3,1,0:T(4,128)S(1)} %get-tuple-element.338), channel_id=1, source_target_pairs={{0,8},{8,16},{16,24},{1,9},{9,17},{17,25},{2,10},{10,18},{18,26},{... | collective-permute-start | bytes 1544 | tf_op jit(solution)/shard_map/ppermute | solution.py:24
  22.5 44.4 %collective-permute-start.9 = (f32[4,1,8,4]{2,3,1,0:T(4,128)S(1)}, f32[4,1,8,4]{2,3,1,0:T(4,128)S(1)}, u32[]{:S(2)}, u32[]{:S(2)}) collective-permute-start(f32[4,1,8,4]{2,3,1,0:T(4,128)S(1)} %get-tuple-element.339), channel_id=1, source_target_pairs={{8,0},{16,8},{24,16},{9,1},{17,9},{25,17},{10,2},{18,10},{26,18},{... | collective-permute-start | bytes 1544 | tf_op jit(solution)/shard_map/ppermute | solution.py:25
  24.8 60.9 %copy-start.94 = (f32[4,8,8,4]{2,3,1,0:T(4,128)}, f32[4,8,8,4]{2,3,1,0:T(4,128)S(1)}, u32[]{:S(2)}) copy-start(f32[4,8,8,4]{2,3,1,0:T(4,128)S(1)} %broadcast_multiply_fusion.2) | copy-start | bytes 12292
  24.8 27.4 %collective-permute-start.4 = (f32[4,1,8,4]{2,3,1,0:T(4,128)S(1)}, f32[4,1,8,4]{2,3,1,0:T(4,128)S(1)}, u32[]{:S(2)}, u32[]{:S(2)}) collective-permute-start(f32[4,1,8,4]{2,3,1,0:T(4,128)S(1)} %get-tuple-element.336), channel_id=1, source_target_pairs={{0,8},{8,16},{16,24},{1,9},{9,17},{17,25},{2,10},{10,18},{18,26},{... | collective-permute-start | bytes 1544 | tf_op jit(solution)/shard_map/ppermute | solution.py:24
  30.4 57.4 %copy-start.96 = (f32[4,8,8,4]{2,3,1,0:T(4,128)}, f32[4,8,8,4]{2,3,1,0:T(4,128)S(1)}, u32[]{:S(2)}) copy-start(f32[4,8,8,4]{2,3,1,0:T(4,128)S(1)} %broadcast_multiply_fusion) | copy-start | bytes 12292
  45.4 111.9 %copy-start.163 = (f32[4,8,8,8]{3,2,1,0:T(8,128)}, f32[4,8,8,8]{3,2,1,0:T(8,128)S(1)}, u32[]{:S(2)}) copy-start(f32[4,8,8,8]{3,2,1,0:T(8,128)S(1)} %get-tuple-element.436) | copy-start | bytes 24580
  46.1 7.3 collective-permute-start.5
  47.4 6.2 collective-permute-start.12
  52.2 5.5 collective-permute-start.13
  57.8 30.0 %collective-permute-start.14 = (f32[4,10,1,4]{2,3,1,0:T(4,128)S(1)}, f32[4,10,1,4]{2,3,1,0:T(4,128)S(1)}, u32[]{:S(2)}, u32[]{:S(2)}) collective-permute-start(f32[4,10,1,4]{2,3,1,0:T(4,128)S(1)} %get-tuple-element.332), channel_id=1, source_target_pairs={{0,1},{1,2},{2,3},{3,4},{4,5},{5,6},{6,7},{8,9},{9,10},{10,11},{11... | collective-permute-start | bytes 1928 | tf_op jit(solution)/shard_map/ppermute | solution.py:24
  59.1 28.7 %collective-permute-start.15 = (f32[4,10,1,4]{2,3,1,0:T(4,128)S(1)}, f32[4,10,1,4]{2,3,1,0:T(4,128)S(1)}, u32[]{:S(2)}, u32[]{:S(2)}) collective-permute-start(f32[4,10,1,4]{2,3,1,0:T(4,128)S(1)} %get-tuple-element.333), channel_id=1, source_target_pairs={{1,0},{2,1},{3,2},{4,3},{5,4},{6,5},{7,6},{9,8},{10,9},{11,10},{12... | collective-permute-start | bytes 1928 | tf_op jit(solution)/shard_map/ppermute | solution.py:25
  60.4 23.8 %collective-permute-start.6 = (f32[4,10,1,4]{2,3,1,0:T(4,128)S(1)}, f32[4,10,1,4]{2,3,1,0:T(4,128)S(1)}, u32[]{:S(2)}, u32[]{:S(2)}) collective-permute-start(f32[4,10,1,4]{2,3,1,0:T(4,128)S(1)} %get-tuple-element.324), channel_id=1, source_target_pairs={{0,1},{1,2},{2,3},{3,4},{4,5},{5,6},{6,7},{8,9},{9,10},{10,11},{11... | collective-permute-start | bytes 1928 | tf_op jit(solution)/shard_map/ppermute | solution.py:24
  66.9 6.8 collective-permute-start.2
  71.0 5.8 collective-permute-start.3
  73.7 6.6 collective-permute-start.10
  76.8 5.2 collective-permute-start.11
  80.3 5.3 collective-permute-start.7
  101.1 833.8 %copy-start.10 = (f32[4,8,8,256]{3,2,1,0:T(8,128)}, f32[4,8,8,256]{3,2,1,0:T(8,128)S(1)}, u32[]{:S(2)}) copy-start(f32[4,8,8,256]{3,2,1,0:T(8,128)S(1)} %get-tuple-element.463) | copy-start | bytes 786436
  179.2 141.1 %copy-start.57 = (f32[4,8,8,8,32]{4,2,1,3,0:T(8,128)}, f32[4,8,8,8,32]{4,2,1,3,0:T(8,128)S(1)}, u32[]{:S(2)}) copy-start(f32[4,8,8,8,32]{4,2,1,3,0:T(8,128)S(1)} %pad_maximum_fusion.3) | copy-start | bytes 786436
  181.3 337.0 %all-reduce.86.cloned.1.call-start = ((), (), s32[]{:S(2)}) async-start(), calls=%async_computation.3 | async-start | bytes 4194304 | tf_op jit(solution)/shard_map/psum | solution.py:265
  354.5 524.9 %copy-start.34 = (f32[4,8,8,256]{3,2,1,0:T(8,128)}, f32[4,8,8,256]{3,2,1,0:T(8,128)S(1)}, u32[]{:S(2)}) copy-start(f32[4,8,8,256]{3,2,1,0:T(8,128)S(1)} %get-tuple-element.475) | copy-start | bytes 786436
  355.3 524.1 %copy-start.369 = (f32[4,8,8]{2,1,0:T(8,128)}, f32[4,8,8]{2,1,0:T(8,128)S(1)}, u32[]{:S(2)}) copy-start(f32[4,8,8]{2,1,0:T(8,128)S(1)} %fusion.625) | copy-start | bytes 3076
  384.5 394.1 %all-reduce.84.cloned.1.call-start = ((), (), s32[]{:S(2)}) async-start(), calls=%async_computation.2 | async-start | bytes 4194304 | tf_op jit(solution)/shard_map/psum | solution.py:272
  644.6 447.8 %all-reduce.82.cloned.1.call-start = ((), (), s32[]{:S(2)}) async-start(), calls=%async_computation.1 | async-start | bytes 4194304 | tf_op jit(solution)/shard_map/psum | solution.py:294
  958.6 422.7 %all-reduce.80.cloned.1.call-start = ((), (), s32[]{:S(2)}) async-start(), calls=%async_computation | async-start | bytes 8126464 | tf_op jit(solution)/shard_map/psum | solution.py:336
  962.4 130.0 %copy-start.47 = (f32[4,8,8,8,32]{4,3,2,1,0:T(8,128)S(1)}, f32[4,8,8,8,32]{4,3,2,1,0:T(8,128)}, u32[]{:S(2)}) copy-start(f32[4,8,8,8,32]{4,3,2,1,0:T(8,128)} %reshape.1270) | copy-start | bytes 786436
  1213.4 92.6 %collective-permute-start.24 = (f32[4,1,8,256]{3,2,1,0:T(8,128)S(1)}, f32[4,1,8,256]{3,2,1,0:T(8,128)S(1)}, u32[]{:S(2)}, u32[]{:S(2)}) collective-permute-start(f32[4,1,8,256]{3,2,1,0:T(8,128)S(1)} %get-tuple-element.294), channel_id=1, source_target_pairs={{0,8},{8,16},{16,24},{1,9},{9,17},{17,25},{2,10},{10,18},{18,26},{... | collective-permute-start | bytes 98312 | tf_op jit(solution)/shard_map/ppermute | solution.py:24
  1216.6 64.8 %collective-permute-start.25 = (f32[4,1,8,256]{3,2,1,0:T(8,128)S(1)}, f32[4,1,8,256]{3,2,1,0:T(8,128)S(1)}, u32[]{:S(2)}, u32[]{:S(2)}) collective-permute-start(f32[4,1,8,256]{3,2,1,0:T(8,128)S(1)} %get-tuple-element.295), channel_id=1, source_target_pairs={{8,0},{16,8},{24,16},{9,1},{17,9},{25,17},{10,2},{18,10},{26,18},{... | collective-permute-start | bytes 98312 | tf_op jit(solution)/shard_map/ppermute | solution.py:25
  1217.9 94.4 %collective-permute-start.16 = (f32[4,1,8,256]{3,2,1,0:T(8,128)S(1)}, f32[4,1,8,256]{3,2,1,0:T(8,128)S(1)}, u32[]{:S(2)}, u32[]{:S(2)}) collective-permute-start(f32[4,1,8,256]{3,2,1,0:T(8,128)S(1)} %get-tuple-element.290), channel_id=1, source_target_pairs={{0,8},{8,16},{16,24},{1,9},{9,17},{17,25},{2,10},{10,18},{18,26},{... | collective-permute-start | bytes 98312 | tf_op jit(solution)/shard_map/ppermute | solution.py:24
  1222.5 86.7 %collective-permute-start.17 = (f32[4,1,8,256]{3,2,1,0:T(8,128)S(1)}, f32[4,1,8,256]{3,2,1,0:T(8,128)S(1)}, u32[]{:S(2)}, u32[]{:S(2)}) collective-permute-start(f32[4,1,8,256]{3,2,1,0:T(8,128)S(1)} %get-tuple-element.291), channel_id=1, source_target_pairs={{8,0},{16,8},{24,16},{9,1},{17,9},{25,17},{10,2},{18,10},{26,18},{... | collective-permute-start | bytes 98312 | tf_op jit(solution)/shard_map/ppermute | solution.py:25
  1223.8 77.2 %collective-permute-start.28 = (f32[4,1,8,256]{3,2,1,0:T(8,128)S(1)}, f32[4,1,8,256]{3,2,1,0:T(8,128)S(1)}, u32[]{:S(2)}, u32[]{:S(2)}) collective-permute-start(f32[4,1,8,256]{3,2,1,0:T(8,128)S(1)} %get-tuple-element.296), channel_id=1, source_target_pairs={{0,8},{8,16},{16,24},{1,9},{9,17},{17,25},{2,10},{10,18},{18,26},{... | collective-permute-start | bytes 98312 | tf_op jit(solution)/shard_map/ppermute | solution.py:24
  1281.4 5.8 collective-permute-start.21
  1287.2 4.3 collective-permute-start.20
  1291.5 6.4 collective-permute-start.29
  1297.9 53.0 %collective-permute-start.22 = (f32[4,10,1,256]{3,2,1,0:T(1,128)S(1)}, f32[4,10,1,256]{3,2,1,0:T(1,128)S(1)}, u32[]{:S(2)}, u32[]{:S(2)}) collective-permute-start(f32[4,10,1,256]{3,2,1,0:T(1,128)S(1)} %get-tuple-element.272), channel_id=1, source_target_pairs={{1,0},{2,1},{3,2},{4,3},{5,4},{6,5},{7,6},{9,8},{10,9},{11,10},{12... | collective-permute-start | bytes 122888 | tf_op jit(solution)/shard_map/ppermute | solution.py:25
  1301.0 49.9 %collective-permute-start.23 = (f32[4,10,1,256]{3,2,1,0:T(1,128)S(1)}, f32[4,10,1,256]{3,2,1,0:T(1,128)S(1)}, u32[]{:S(2)}, u32[]{:S(2)}) collective-permute-start(f32[4,10,1,256]{3,2,1,0:T(1,128)S(1)} %get-tuple-element.273), channel_id=1, source_target_pairs={{0,1},{1,2},{2,3},{3,4},{4,5},{5,6},{6,7},{8,9},{9,10},{10,11},{11... | collective-permute-start | bytes 122888 | tf_op jit(solution)/shard_map/ppermute | solution.py:24
  1306.0 37.4 %collective-permute-start.30 = (f32[4,10,1,256]{3,2,1,0:T(1,128)S(1)}, f32[4,10,1,256]{3,2,1,0:T(1,128)S(1)}, u32[]{:S(2)}, u32[]{:S(2)}) collective-permute-start(f32[4,10,1,256]{3,2,1,0:T(1,128)S(1)} %get-tuple-element.280), channel_id=1, source_target_pairs={{1,0},{2,1},{3,2},{4,3},{5,4},{6,5},{7,6},{9,8},{10,9},{11,10},{12... | collective-permute-start | bytes 122888 | tf_op jit(solution)/shard_map/ppermute | solution.py:25
  1309.2 9.6 collective-permute-start.26
  1312.3 7.8 collective-permute-start.27
  1318.8 13.1 collective-permute-start.18
  1320.1 15.7 %collective-permute-start.19 = (f32[4,10,1,256]{3,2,1,0:T(1,128)S(1)}, f32[4,10,1,256]{3,2,1,0:T(1,128)S(1)}, u32[]{:S(2)}, u32[]{:S(2)}) collective-permute-start(f32[4,10,1,256]{3,2,1,0:T(1,128)S(1)} %get-tuple-element.269), channel_id=1, source_target_pairs={{0,1},{1,2},{2,3},{3,4},{4,5},{5,6},{6,7},{8,9},{9,10},{10,11},{11... | collective-permute-start | bytes 122888 | tf_op jit(solution)/shard_map/ppermute | solution.py:24
  1331.9 11.4 collective-permute-start.31
  (511 other events, 1357.5 us)
Sparse Core Ops, SparseCore 0:
  181.4 138.7 all-reduce.87
  384.6 133.6 all-reduce.85
  644.7 133.7 all-reduce.83
  958.7 133.6 all-reduce.81
  1233.8 147.4 all-reduce.79
where the time goes:
time: 1420 us; the launch traced here: 1400 us
  waiting for transfers between devices  536 us (38%)
  matrix products  410 us (29%)
  local copies, waits for them, and re-layouts  233 us (16%)
  starting transfers between devices  83.3 us (6%)
  other arithmetic  78.2 us (6%)
  blocking collectives  40.6 us (3%)
  between operations  19.7 us (1%)
    dot_general x140, matrix products, matmul(): return jnp.matmul(left, right, precision=highest)  179 us
    psum x1, waiting for transfers between devices, body(): lax.psum(summary(key_heads, value_heads, weight), ('row', 'col'))  132 us
    psum x1, waiting for transfers between devices, body(): dec_grad = lax.psum(dec_part, ('row', 'col'))  131 us
    psum x1, waiting for transfers between devices, body(): kv_grad = lax.psum(kv_part, ('row', 'col'))  129 us
    psum x1, waiting for transfers between devices, body(): lax.psum(decode_summary(pair_params, hidden2, weight), ('row', 'col'))  126 us
    reshape x48, local copies, waits for them, and re-layouts, split_heads(): return values.reshape(values.shape[:-1] + (HEADS, HEAD))  77.9 us
    dot_general x36, matrix products, conv_transpose(): jnp.einsum('brco,io->brci', window, weight_in[shift_row, shift_col], prec...  66.4 us
    ppermute x16, starting transfers between devices, padded_2(): before = lax.ppermute(last, axis, up)  61.9 us
  transfers between devices with their start and end apart: 37, of which 10 were waited for; matrix products, arithmetic and copies ran while one was open for 8% of the time, Pallas kernels for 0%

commit v1 on v0

--- a/solution.py
+++ b/solution.py
@@ -1,17 +1,20 @@
 import math
+import types
 
 import jax
 import jax.numpy as jnp
 from jax import lax
+from jax.experimental import pallas as pl
+from jax.experimental.pallas import tpu as pltpu
 from jax.sharding import PartitionSpec as P
 
 HEADS = 8
 HEAD = 32
 FOUR = 128
-MICRO = 4
-
 
 highest = lax.Precision.HIGHEST
+f32 = jnp.float32
+MESH = pl.DeviceIdType.MESH
 
 
 def padded_2(x, sides, width):
@@ -188,13 +191,7 @@
     return result * inside[..., None]
 
 
-def accumulate(running, fresh):
-    if running is None:
-        return fresh
-    return jax.tree.map(lambda left, right: left + right, running, fresh)
-
-
-def body(
+def general_body(
     field_in,
     conv_weight,
     conv_bias,
@@ -221,9 +218,9 @@
     cotangent,
     grid_sizes,
 ):
+    both = ("row", "col")
     tile_rows = field_in.shape[1]
     tile_cols = field_in.shape[2]
-    per_items = field_in.shape[0] // MICRO
     row_index = lax.axis_index("row") * tile_rows + jnp.arange(tile_rows, dtype=jnp.int32)
     col_index = lax.axis_index("col") * tile_cols + jnp.arange(tile_cols, dtype=jnp.int32)
     front_params = (first_gain, first_shift, query_weight, key_weight, value_weight)
@@ -245,182 +242,1030 @@
         propagate_down,
         propagate_shift,
     )
-    decoder_total = None
-    encoder_total = None
-    results = []
-    field_grads = []
-    for micro in range(MICRO):
-        first_item = micro * per_items
-        field_part = field_in[first_item : first_item + per_items]
-        cot_part = cotangent[first_item : first_item + per_items]
-        sizes_part = grid_sizes[first_item : first_item + per_items]
-        inside, coord_x, coord_y, points = geometry(row_index, col_index, sizes_part)
-        fourier = features(coord_x, coord_y)
-        weight = inside / points[:, None, None]
-        padded = padded_2(field_part * inside[..., None], (("row", 1), ("col", 2)), 1)
-        hidden0 = conv_embed(padded, conv_weight, conv_bias)
-        query_heads, key_heads, value_heads = project(front_params, hidden0, coord_x, coord_y)
-        kv_summary = lax.psum(summary(key_heads, value_heads, weight), ("row", "col"))
-        hidden2 = encoder_rest(rest_params, hidden0, query_heads, kv_summary)
-        dec_summary = lax.psum(decode_summary(pair_params, hidden2, weight), ("row", "col"))
-
-        def decode_local(params, summary_in):
-            return decode_out(params, fourier, summary_in, inside)
-
-        result, out_back = jax.vjp(decode_local, out_params, dec_summary)
-        out_grads, dec_part = out_back(cot_part)
-        dec_grad = lax.psum(dec_part, ("row", "col"))
-
-        def pair_local(params, hidden_in):
-            return decode_summary(params, hidden_in, weight)
-
-        pair_back = jax.vjp(pair_local, pair_params, hidden2)[1]
-        pair_grads, hidden2_grad = pair_back(dec_grad)
-        decoder_total = accumulate(
-            decoder_total,
-            (
-                out_grads[0],
-                pair_grads[0],
-                pair_grads[1],
-                out_grads[1],
-                out_grads[2],
-                out_grads[3],
-                out_grads[4],
-                out_grads[5],
-            ),
+    inside, coord_x, coord_y, points = geometry(row_index, col_index, grid_sizes)
+    fourier = features(coord_x, coord_y)
+    weight = inside / points[:, None, None]
+    padded = padded_2(field_in * inside[..., None], (("row", 1), ("col", 2)), 1)
+    hidden0 = conv_embed(padded, conv_weight, conv_bias)
+    query_heads, key_heads, value_heads = project(front_params, hidden0, coord_x, coord_y)
+    kv_summary = lax.psum(summary(key_heads, value_heads, weight), both)
+    hidden2 = encoder_rest(rest_params, hidden0, query_heads, kv_summary)
+    dec_summary = lax.psum(decode_summary(pair_params, hidden2, weight), both)
+
+    def decode_local(params, summary_in):
+        return decode_out(params, fourier, summary_in, inside)
+
+    result, out_back = jax.vjp(decode_local, out_params, dec_summary)
+    out_grads, dec_part = out_back(cotangent)
+    dec_grad = lax.psum(dec_part, both)
+
+    def pair_local(params, hidden_in):
+        return decode_summary(params, hidden_in, weight)
+
+    pair_grads, hidden2_grad = jax.vjp(pair_local, pair_params, hidden2)[1](dec_grad)
+    rest_back = jax.vjp(encoder_rest, rest_params, hidden0, query_heads, kv_summary)[1]
+    rest_grads, hidden0_part, query_grad, kv_part = rest_back(hidden2_grad)
+    kv_grad = lax.psum(kv_part, both)
+
+    def summary_local(key_in, value_in):
+        return summary(key_in, value_in, weight)
+
+    key_grad, value_grad = jax.vjp(summary_local, key_heads, value_heads)[1](kv_grad)
+
+    def project_local(params, hidden_in):
+        return project(params, hidden_in, coord_x, coord_y)
+
+    front_grads, hidden0_more = jax.vjp(project_local, front_params, hidden0)[1](
+        (query_grad, key_grad, value_grad)
+    )
+    hidden0_grad = hidden0_part + hidden0_more
+
+    def conv_local(weight_in, bias_in):
+        return conv_embed(padded, weight_in, bias_in)
+
+    conv_grads = jax.vjp(conv_local, conv_weight, conv_bias)[1](hidden0_grad)
+    grad_padded = padded_2(hidden0_grad, (("row", 1), ("col", 2)), 1)
+    field_grad = conv_transpose(grad_padded, conv_weight) * inside[..., None]
+    totals = lax.psum(
+        (
+            *conv_grads,
+            *front_grads,
+            *rest_grads,
+            out_grads[0],
+            *pair_grads,
+            *out_grads[1:],
+        ),
+        both,
+    )
+    return (result, field_grad, *totals)
+
+
+NT = 8
+ITEMS = 16
+ROWS, COLS = 4, 8
+DEVICES = ROWS * COLS
+PTS = 1024
+D = 256
+
+CHUNKS = ((0, 512, 1), (512, 512, 1), (1024, 512, 1), (1536, 512, 1), (2048, 512, 1), (2560, 512, 1), (3072, 512, 1), (3584, 256, 1), (3840, 256, 1))
+R_UP, R_DOWN = 0, 512
+R_DO, R_DQ, R_DK, R_DV = 1024, 1280, 1536, 1792
+R_RET, R_HID, R_O, R_Q, R_V, R_K = 2048, 2560, 3072, 3328, 3584, 3840
+G_ROWS = 4096
+VECS = ("cb", "g1", "s1", "g2", "s2", "br", "ps", "bh", "bu")
+SMALL = 8 * DEVICES
+S_CONV, S_VEC = 0, 144
+PLAN = ((), (), (0,), (1,), (), (), (), (), (), (), (2, 1), (), (), (), (), (0, 3), (), (), (4, 1), (5,), (3, 0), (), (2,), (), (1, 4), (), (6, 5), (2,), (0, 3, 1), (8,), (), (2, 4), (7, 5, 0, 4, 0, 8), ())
+TAIL = (6, 1, 5, 2, 6, 7, 3, 8, 4, -1, 4, 6, 7, 8, 7, 3, 8, 8, -2, 5, 6, 3, 7, 6, 2, 5, 7)
+AXES, PLANE, ALL = range(3)
+SEMS = 32
+
+
+def dot(a, b, ca, cb):
+    return lax.dot_general(a, b, (((ca,), (cb,)), ((), ())), preferred_element_type=f32)
+
+
+def cut(x):
+    top = x.astype(jnp.bfloat16)
+    return top, (x - top.astype(f32)).astype(jnp.bfloat16)
+
+
+def dot3(a, b, ca, cb):
+    (a0, a1), (b0, b1) = cut(a), cut(b)
+    return dot(a0, b0, ca, cb) + (dot(a0, b1, ca, cb) + dot(a1, b0, ca, cb))
+
+
+def nn(a, b):
+    return dot3(a, b, 1, 0)
+
+
+def nt(a, b):
+    return dot3(a, b, 1, 1)
+
+
+def tn(a, b):
+    return dot3(a, b, 0, 0)
+
+
+def dot_mark(e, b, ca):
+    b0, b1 = cut(b)
+    return dot(e, b0, ca, 0) + dot(e, b1, ca, 0)
+
+
+def iota(shape, dim):
+    return lax.broadcasted_iota(jnp.int32, shape, dim)
+
+
+GC = math.sqrt(2.0 / math.pi)
+
+
+def gelu_both(x):
+    x2 = x * x
+    t = jnp.tanh(GC * (x + 0.044715 * (x2 * x)))
+    half = 0.5 * (1.0 + t)
+    slope = half + 0.5 * x * (1.0 - t * t) * (GC + (3 * 0.044715 * GC) * x2)
+    return x * half, slope
+
+
+def turn_sin(u):
+    return jnp.sin((2.0 * math.pi) * (u - jnp.round(u)))
+
+
+def compact(z):
+    lane = iota((HEAD, D), 1) // HEAD
+    total = jnp.zeros((HEAD, D), f32)
+    for h in range(HEADS):
+        total = total + jnp.where(lane == h, z[h * HEAD : (h + 1) * HEAD, :], 0.0)
+    return total
+
+
+def expand(blocks):
+    lane = iota((HEAD, D), 1) // HEAD
+    return jnp.concatenate([jnp.where(lane == h, blocks, 0.0) for h in range(HEADS)], axis=0)
+
+
+def swap_pairs(v):
+    parts = []
+    for s in range(D // 128):
+        part = v[:, s * 128 : (s + 1) * 128]
+        low = (iota(part.shape, 1) // 8) % 2 == 0
+        parts.append(jnp.where(low, pltpu.roll(part, 120, 1), pltpu.roll(part, 8, 1)))
+    return jnp.concatenate(parts, axis=1)
+
+
+def norm_back(dn, nhat, rstd):
+    a = jnp.mean(dn, axis=-1, keepdims=True)
+    b = jnp.mean(dn * nhat, axis=-1, keepdims=True)
+    return rstd * (dn - a - nhat * b)
+
+
+def colsum(v):
+    return jnp.sum(v, axis=0, keepdims=True)
+
+
+def shift_cols(f, step):
+    if step == 0:
+        return f
+    n = f.shape[1]
+    lane = iota(f.shape, 1)
+    col, tile = lane % 8, (lane // 64) % 8
+    if step == 1:
+        near, far = pltpu.roll(f, n - 1, 1), pltpu.roll(f, n - 57, 1)
+        return jnp.where(col < 7, near, jnp.where(tile < COLS - 1, far, 0.0))
+    near, far = pltpu.roll(f, 1, 1), pltpu.roll(f, 57, 1)
+    return jnp.where(col > 0, near, jnp.where(tile > 0, far, 0.0))
+
+
+def shift_rows(f, step):
+    if step == 0:
+        return f
+    n = f.shape[1]
+    lane = iota(f.shape, 1)
+    row, tile = (lane // 8) % 8, lane // 512
+    if step == 1:
+        near, far = pltpu.roll(f, n - 8, 1), pltpu.roll(f, n - 456, 1)
+        return jnp.where(row < 7, near, jnp.where(tile < ROWS - 1, far, 0.0))
+    near, far = pltpu.roll(f, 8, 1), pltpu.roll(f, 456, 1)
+    return jnp.where(row > 0, near, jnp.where(tile > 0, far, 0.0))
+
+
+INPUTS = dict(
+    fld=(NT * NT, 4, ITEMS),
+    ct=(PTS, D),
+    wc=(9, 4, D),
+    cb=(1, D),
+    g1=(1, D),
+    s1=(1, D),
+    wq=(D, D),
+    wk=(D, D),
+    wv=(D, D),
+    wo=(D, D),
+    g2=(1, D),
+    s2=(1, D),
+    wh=(D, 512),
+    bh=(1, 512),
+    wr=(512, D),
+    br=(1, D),
+    dq=(128, D),
+    dk=(D, D),
+    dv=(D, D),
+    do=(D, D),
+    wu=(D, 512),
+    bu=(1, 512),
+    wd=(512, D),
+    ps=(1, D),
+)
+
+
+def kernel(*refs):
+    gs, *refs = refs
+    args, refs = refs[: len(INPUTS)], refs[len(INPUTS) :]
+    o_res, o_fg, o_small, o_g, *refs = refs
+    R = types.SimpleNamespace(**dict(zip([*SCRATCH, *INPUTS], refs, strict=True)))
+    G = R.G
+    row, col = lax.axis_index("row"), lax.axis_index("col")
+    me = row * COLS + col
+    core, xbit, ybit = col % 2, (col // 2) % 2, col // 4
+    item = me // 2
+
+    def at(number):
+        return (number // COLS, number % COLS)
+
+    def remote(src, dst, send, recv, to):
+        copy = pltpu.make_async_remote_copy(
+            src_ref=src, dst_ref=dst, send_sem=send, recv_sem=recv, device_id=to, device_id_type=MESH
         )
-        rest_back = jax.vjp(encoder_rest, rest_params, hidden0, query_heads, kv_summary)[1]
-        rest_grads, hidden0_part, query_grad, kv_part = rest_back(hidden2_grad)
-        kv_grad = lax.psum(kv_part, ("row", "col"))
-
-        def summary_local(key_in, value_in):
-            return summary(key_in, value_in, weight)
-
-        key_grad, value_grad = jax.vjp(summary_local, key_heads, value_heads)[1](kv_grad)
-
-        def project_local(params, hidden_in):
-            return project(params, hidden_in, coord_x, coord_y)
-
-        front_grads, hidden0_more = jax.vjp(project_local, front_params, hidden0)[1](
-            (query_grad, key_grad, value_grad)
+        copy.start()
+        return copy
+
+    def drain(ref, sem):
+        pltpu.make_async_copy(ref, ref, sem).wait()
+
+    def send_or_copy(src, dst, send, recv, number):
+        @pl.when(number != me)
+        def _():
+            remote(src, dst, send, recv, at(number))
+
+        @pl.when(number == me)
+        def _():
+            pltpu.make_async_copy(src, dst, recv).start()
+
+    loads = {}
+    for i, n in enumerate(INPUTS):
+        loads[n] = pltpu.make_async_copy(args[i], getattr(R, n), R.s_in.at[i])
+        loads[n].start()
+
+    def need(*wanted):
+        for n in wanted:
+            loads.pop(n).wait()
+
+    barrier = pltpu.get_barrier_semaphore()
+    for k in range(1, DEVICES):
+        pl.semaphore_signal(
+            barrier, inc=1, device_id=at((me + k) % DEVICES), device_id_type=MESH
         )
-        hidden0_grad = hidden0_part + hidden0_more
-
-        def conv_local(weight_in, bias_in):
-            return conv_embed(padded, weight_in, bias_in)
-
-        conv_grads = jax.vjp(conv_local, conv_weight, conv_bias)[1](hidden0_grad)
-        grad_padded = padded_2(hidden0_grad, (("row", 1), ("col", 2)), 1)
-        field_grad = conv_transpose(grad_padded, conv_weight) * inside[..., None]
-        encoder_total = accumulate(
-            encoder_total,
-            (
-                conv_grads[0],
-                conv_grads[1],
-                front_grads[0],
-                front_grads[1],
-                front_grads[2],
-                front_grads[3],
-                front_grads[4],
-                rest_grads[0],
-                rest_grads[1],
-                rest_grads[2],
-                rest_grads[3],
-                rest_grads[4],
-                rest_grads[5],
-                rest_grads[6],
-            ),
+
+    need("fld")
+    for ch in range(4):
+        R.FA[pl.ds(ch, ITEMS, stride=8), pl.ds(0, 64)] = jnp.transpose(R.fld[:, ch, :])
+    size_r, size_c = gs[0, item], gs[1, item]
+    fr, fc = size_r.astype(f32), size_c.astype(f32)
+
+    def rotary_tables():
+        shape = (80, 128)
+        k, lane = iota(shape, 0), iota(shape, 1)
+        is_x = k < 16
+        coord = jnp.where(
+            is_x,
+            ((16 * core + k).astype(f32) + 0.5) / fr,
+            ((k - 16).astype(f32) + 0.5) / fc,
         )
-        results.append(result)
-        field_grads.append(field_grad)
-    totals = lax.psum(tuple(encoder_total) + tuple(decoder_total), ("row", "col"))
-    result_field = jnp.concatenate(results, axis=0)
-    field_grad_all = jnp.concatenate(field_grads, axis=0)
+        freq = (lane % 8 + 1).astype(f32)
+        quarter = (lane // 8) % 4
+        keep = is_x == (quarter < 2)
+        turns = freq * coord
+        turns = turns - jnp.round(turns)
+        cos_t = jnp.where(keep, turn_sin(turns + 0.25), 0.0)
+        sin_t = jnp.where(keep, turn_sin(turns), 0.0)
+        sin_t = jnp.where(quarter % 2 == 0, -sin_t, sin_t)
+        p, t = iota((PTS, 80), 0), iota((PTS, 80), 1)
+        pick = (t == 8 * (p // 512) + (p // 8) % 8) | (t - 16 == 8 * ((p // 64) % 8) + p % 8)
+        R.rot[...] = dot_mark(
+            pick.astype(jnp.bfloat16), jnp.concatenate([cos_t, sin_t], axis=1), 1
+        )
+
+    def fourier_tables():
+        shape = (96, 128)
+        k, lane = iota(shape, 0), iota(shape, 1)
+        is_x = k < 32
+        coord = jnp.where(is_x, (k.astype(f32) + 0.5) / fr, ((k - 32).astype(f32) + 0.5) / fc)
+        turns = 0.5 * ((lane % 32 + 1).astype(f32) * coord)
+        turns = turns - jnp.round(turns)
+        turns = jnp.where((lane // 32) % 2 == 0, turns, turns + 0.25)
+        R.FF[...] = jnp.where(is_x == (lane < 64), turn_sin(turns), 0.0)
+
+    def tile_masks():
+        p = iota((PTS, 128), 0)
+        here_r = 16 * core + 8 * (p // 512) + (p // 8) % 8
+        here_c = 8 * ((p // 64) % 8) + p % 8
+        inv_points = 1.0 / (fr * fc)
+        R.wgt[...] = jnp.where((here_r < size_r) & (here_c < size_c), inv_points, 0.0)
+        for b in range(ITEMS):
+            p = iota((64, 128), 0)
+            ok = (NT * row + (p // 8) % 8 < gs[0, b]) & (NT * col + p % 8 < gs[1, b])
+            R.mask[pl.ds(64 * b, 64)] = ok.astype(f32)
+        p, t = iota((PTS, D), 0), iota((PTS, D), 1)
+        chosen = (p // 64 == t // 16) & (
+            ((t % 16) == (p // 8) % 8) | ((t % 16) == 8 + p % 8)
+        )
+        R.E[...] = chosen.astype(jnp.bfloat16)
+
+    rotary_tables()
+    fourier_tables()
+    tile_masks()
+    need("ct", "wd")
+    mask2 = jnp.concatenate([R.mask[...]] * 2, axis=1)
+    R.ctm[...] = R.ct[...] * mask2
+    need("wc")
+    R.W9[...] = jnp.zeros((72, D), f32)
+    for k in range(9):
+        R.W9[pl.ds(8 * k, 4)] = R.wc[k]
+    pl.semaphore_wait(barrier, DEVICES - 1)
+
+    for k in range(1, DEVICES):
+        to = (me + k) % DEVICES
+        remote(
+            R.FA.at[pl.ds((to // 2) * 8, 4)],
+            R.FR.at[pl.ds(me * 8, 4)],
+            R.s_f.at[0],
+            R.r_f.at[0],
+            at(to),
+        )
+    R.FR[pl.ds(me * 8, 4)] = R.FA[pl.ds(item * 8, 4)]
+
+    R.dact[...] = nt(R.ctm[...], R.wd[...])
+    R.rcc[...] = dot_mark(R.E[...], R.ctm[...], 0)
+    ps_grad = colsum(R.ctm[...])
+
+    def cossin():
+        c, s = R.rot[:, :128], R.rot[:, 128:]
+        return jnp.concatenate([c, c], axis=1), jnp.concatenate([s, s], axis=1)
+
+    def turn(v):
+        c, s = cossin()
+        return v * c + swap_pairs(v) * s
+
+    def turn_back(v):
+        c, s = cossin()
+        return v * c - swap_pairs(v) * s
+
+    def wgt2():
+        return jnp.concatenate([R.wgt[...]] * 2, axis=1)
+
+    need(*list(loads))
+    drain(R.FR.at[pl.ds(0, 4 * (DEVICES - 1))], R.r_f.at[0])
+    lane, sub = iota((8, DEVICES * 64), 1), iota((8, DEVICES * 64), 0)
+    full_r, full_c = 8 * (lane // 512) + (lane // 8) % 8, 8 * ((lane // 64) % 8) + lane % 8
+    full_mask = (full_r < size_r) & (full_c < size_c) & (sub < 4)
+    low = iota((8, 128), 1) < 64
+    pieces = []
+    for k in range(DEVICES // 2):
+        left = R.FR[pl.ds(16 * k, 8)]
+        right = R.FR[pl.ds(16 * k + 8, 8)]
+        pieces.append(jnp.where(low, left, pltpu.roll(right, 64, 1)))
+    field = jnp.where(full_mask, jnp.concatenate(pieces, axis=1), 0.0)
+    for dj in range(3):
+        along = shift_cols(field, dj - 1)
+        for di in range(3):
+            patch = shift_rows(along, di - 1)
+            mine = jnp.where(core == 0, patch[:, :PTS], patch[:, PTS:])
+            R.PT[pl.ds((di * 3 + dj) * 8, 8)] = mine
+
+    hidden0 = tn(R.PT[...], R.W9[...]) + R.cb[...]
+    R.h0[...] = hidden0
+    mean = jnp.mean(hidden0, axis=-1, keepdims=True)
+    center = hidden0 - mean
+    rstd1 = lax.rsqrt(jnp.mean(center * center, axis=-1, keepdims=True) + 1e-5)
+    R.rs1[...] = jnp.broadcast_to(rstd1, (PTS, 128))
+    R.n1[...] = center * rstd1
+    R.n[...] = R.n1[...] * R.g1[...] + R.s1[...]
+    R.k[...] = turn(nn(R.n[...], R.wk[...]))
+    R.wn[...] = R.n[...] * wgt2()
+    R.T[...] = tn(R.k[...], R.wn[...])
+
+    pair = (row, col + 1 - 2 * core)
+
+    def swap_start(i, value):
+        R.XS[i] = value
+        return remote(R.XS.at[i], R.XR.at[i], R.s_x.at[i], R.r_x.at[i], pair)
+
+    def swap_end(i, copy):
+        copy.wait()
+        return R.XS[i] + R.XR[i]
+
+    going = swap_start(0, compact(nn(R.T[...], R.wv[...])))
+    R.q[...] = turn(nn(R.n[...], R.wq[...]))
+    R.KV[...] = expand(swap_end(0, going))
+    R.KVO[...] = nn(R.KV[...], R.wo[...])
+    hidden1 = R.h0[...] + nn(R.q[...], R.KVO[...])
+    mean = jnp.mean(hidden1, axis=-1, keepdims=True)
+    center = hidden1 - mean
+    rstd2 = lax.rsqrt(jnp.mean(center * center, axis=-1, keepdims=True) + 1e-5)
+    R.rs2[...] = jnp.broadcast_to(rstd2, (PTS, 128))
+    R.m1[...] = center * rstd2
+    R.m[...] = R.m1[...] * R.g2[...] + R.s2[...]
+    R.h1[...] = hidden1 + R.br[...]
+    a, slope = gelu_both(nn(R.m[...], R.wh[...]) + R.bh[...])
+    R.a[...] = a
+    R.az[...] = slope
+    R.h2[...] = R.h1[...] + nn(R.a[...], R.wr[...])
+    R.gram[...] = tn(R.h2[...], R.h2[...] * wgt2())
+    half = nn(tn(R.dk[...], R.gram[...]), R.dv[...])
+    going = swap_start(1, compact(half))
+    R.DS[...] = expand(swap_end(1, going))
+    R.P1[...] = nn(R.dq[...], R.DS[...])
+    R.AB[...] = nn(R.FF[...], nn(R.P1[...], R.do[...]))
+
+    for k in range(16):
+        R.TS[k, pl.ds(0, 8)] = R.AB[pl.ds(16 * core + 8 * (k // 8), 8)]
+        R.TS[k, pl.ds(8, 8)] = R.AB[pl.ds(32 + 8 * (k % 8), 8)]
+    for k in range(16):
+        slot = (me + k) % 16
+        send_or_copy(
+            R.TS.at[slot],
+            R.TR.at[item],
+            R.s_t.at[0],
+            R.r_t.at[item],
+            16 * core + slot,
+        )
+    for b in range(ITEMS):
+        drain(R.TR.at[b], R.r_t.at[b])
+
+    first, second = (
+        xbit * (1 - core) + ybit * core,
+        ybit * (1 - core) + xbit * core,
+    )
+    step_x, step_y = 2 - 4 * xbit, 4 - 8 * ybit
+    col_first = col + step_x * (1 - core) + step_y * core
+    col_second = col + step_y * (1 - core) + step_x * core
+
+    def sum_chunk(i):
+        o, n, kind = CHUNKS[i]
+        buf, used, free = R.RB, [SEMS * i], [o]
+        place = 2 * ybit + xbit
+        half_at = o + core * (n // 2)
+        quarter_at = half_at + first * (n // 4)
+        eighth_at = quarter_at + second * (n // 8) if kind == AXES else half_at + place * (n // 8)
+        shard_at = eighth_at + row * (n // 32)
+        plane = [
+            (row, col + step_x, 2 * ybit + 1 - xbit),
+            (row, col + step_y, 2 * (1 - ybit) + xbit),
+            (row, col + step_x + step_y, 2 * (1 - ybit) + 1 - xbit),
+        ]
+        here = (row, col, place)
+        line = [((row + z) % ROWS, col) for z in range(1, ROWS)]
+
+        def part(ref, start, count):
+            return ref.at[pl.ds(pl.multiple_of(start, 8), count)]
+
+        def go(src, dst, to):
+            copy = remote(src, dst, R.s_g.at[used[0]], R.r_g.at[used[0]], to)
+            used[0] += 1
+            return copy
+
+        def give(mine, count, *away):
+            copies, came = [], []
+            for start, to in away:
+                here = buf.at[pl.ds(free[0], count)]
+                free[0] += count
+                came.append(here)
+                copies.append(go(part(G, start, count), here, to))
+
+            def add(into):
+                for copy in copies:
+                    copy.wait()
+                total = part(G, mine, count)[...]
+                for here in came:
+                    total = total + here[...]
+                part(into, mine, count)[...] = total
+
+            return add
+
+        def spread(mine, count, *to):
+            rows = part(R.SUM, mine, count)
+            copies = [go(rows, rows, device) for device in to]
+
+            def wait():
+                for copy in copies:
+                    copy.wait()
+
+            return wait
+
+        add = give(half_at, n // 2, (o + (1 - core) * (n // 2), pair))
+        yield
+        add(G)
+        if kind == ALL:
+            chips = [((row + z) % ROWS, c, p) for z in range(ROWS) for _, c, p in [here, *plane]][1:]
+            away = [(half_at + (4 * p + r) * (n // 32), (r, c)) for r, c, p in chips]
+            shard_at = half_at + (4 * place + row) * (n // 32)
+            add = give(shard_at, n // 32, *away)
+            yield
+            add(R.SUM)
+            wait = spread(shard_at, n // 32, *[(r, c) for r, c, _ in chips])
+            yield
+            wait()
+        elif kind == PLANE:
+            away = [(half_at + p * (n // 8), (r, c)) for r, c, p in plane]
+            add = give(eighth_at, n // 8, *away)
+            yield
+            add(G)
+        else:
+            away = half_at + (1 - first) * (n // 4)
+            add = give(quarter_at, n // 4, (away, (row, col_first)))
+            yield
+            add(G)
+            away = quarter_at + (1 - second) * (n // 8)
+            add = give(eighth_at, n // 8, (away, (row, col_second)))
+            yield
+            add(G)
+        if kind != ALL:
+            away = [(eighth_at + to[0] * (n // 32), to) for to in line]
+            add = give(shard_at, n // 32, *away)
+            yield
+            add(R.SUM)
+            wait = spread(shard_at, n // 32, *line)
+            yield
+            wait()
+        if kind == PLANE:
+            wait = spread(eighth_at, n // 8, *[(r, c) for r, c, _ in plane])
+            yield
+            wait()
+        elif kind == AXES:
+            wait = spread(eighth_at, n // 8, (row, col_second))
+            yield
+            wait()
+            wait = spread(quarter_at, n // 4, (row, col_first))
+            yield
+            wait()
+        wait = spread(half_at, n // 2, pair)
+        yield
+        wait()
+        out = pltpu.make_async_copy(
+            R.SUM.at[pl.ds(o, n)], o_g.at[pl.ds(o, n)], R.s_o.at[1 + i]
+        )
+        out.start()
+        outs.append(out)
+
+    going_on, outs, plan = {}, [], list(PLAN)
+
+    def launch(*ready):
+        for i, chunk in enumerate(CHUNKS):
+            if chunk[0] in ready:
+                going_on[i] = sum_chunk(i)
+                next(going_on[i])
+        step()
+
+    def advance(i):
+        if next(going_on[i], i) == i:
+            del going_on[i]
+
+    def step():
+        for i in plan.pop(0):
+            advance(i)
+
+    table = R.TR[...].reshape(ITEMS * 16, D)
+    R.UT[...] = nn(table, R.wu[...])
+    a, slope = gelu_both(dot_mark(R.E[...], R.UT[...], 1) + R.bu[...])
+    R.act[...] = a
+    R.dpre[...] = slope * R.dact[...]
+    R.rc[...] = dot_mark(R.E[...], R.dpre[...], 0)
+    R.DAB[...] = (nt(R.rc[...], R.wu[...]) + R.rcc[...]).reshape(ITEMS, 16, D)
+    for k in range(ITEMS):
+        b = (item + k) % ITEMS
+        send_or_copy(
+            R.DAB.at[b],
+            R.DR.at[me % 16],
+            R.s_r.at[0],
+            R.r_r.at[me % 16],
+            2 * b + row // 2,
+        )
+    table = R.TR[...].reshape(ITEMS * 16, D)
+    grad = tn(table, R.rc[...])
+    G[pl.ds(R_UP, D)] = grad[:, :D]
+    G[pl.ds(R_UP + D, D)] = grad[:, D:]
+    launch(R_UP)
+    G[pl.ds(R_DOWN, 512)] = tn(R.act[...], R.ctm[...])
+    step()
+    launch(R_DOWN)
+    latent = dot_mark(R.E[...], table, 1)
+    mask2 = jnp.concatenate([R.mask[...]] * 2, axis=1)
+    R.res[...] = (latent + nn(R.act[...], R.wd[...]) + R.ps[...]) * mask2
+    out_res = pltpu.make_async_copy(R.res, o_res, R.s_o.at[0])
+    out_res.start()
+    bu_grad = colsum(R.dpre[...])
+    step()
+
+    for k in range(16):
+        drain(R.DR.at[k], R.r_r.at[k])
+    step()
+    da = [jnp.zeros((8, D), f32) for _ in range(2)]
+    db = []
+    for t in range(COLS):
+        for s in range(2):
+            da[s] = da[s] + R.DR[s * 8 + t, pl.ds(0, 8)]
+        db.append(R.DR[t, pl.ds(8, 8)] + R.DR[8 + t, pl.ds(8, 8)])
+    zero = jnp.zeros((8, D), f32)
+    is0 = core == 0
+    dab = jnp.concatenate(
+        [
+            jnp.where(is0, da[0], zero),
+            jnp.where(is0, da[1], zero),
+            jnp.where(is0, zero, da[0]),
+            jnp.where(is0, zero, da[1]),
+            *db,
+        ],
+        axis=0,
+    )
+    dm_table = tn(R.FF[...], dab)
+    dp1 = nt(dm_table, R.do[...])
+    going = swap_start(2, compact(tn(R.dq[...], dp1)))
+    step()
+    G[pl.ds(R_DO, D)] = tn(R.P1[...], dm_table)
+    G[pl.ds(R_DQ, 128)] = nt(dp1, R.DS[...])
+    G[pl.ds(R_DQ + 128, 128)] = jnp.zeros((128, D), f32)
+    step()
+    launch(R_DO)
+    x2 = nn(R.gram[...], R.dv[...])
+    step()
+    dd = expand(swap_end(2, going))
+    step()
+    y1 = nn(R.dk[...], dd)
+    dgram = nt(y1, R.dv[...]) + nt(R.dv[...], y1)
+    step()
+    R.dh[...] = nn(R.h2[...], dgram) * wgt2()
+    step()
+    G[pl.ds(R_DK, D)] = nt(x2, dd)
+    G[pl.ds(R_DV, D)] = tn(R.gram[...], y1)
+    step()
+    launch(R_DK)
+    br_grad = colsum(R.dh[...])
+    G[pl.ds(R_RET, 512)] = tn(R.a[...], R.dh[...])
+    step()
+    launch(R_RET)
+    R.dz[...] = nt(R.dh[...], R.wr[...]) * R.az[...]
+    bh_grad = colsum(R.dz[...])
+    step()
+    grad = tn(R.m[...], R.dz[...])
+    G[pl.ds(R_HID, D)] = grad[:, :D]
+    G[pl.ds(R_HID + D, D)] = grad[:, D:]
+    step()
+    launch(R_HID)
+    dm = nt(R.dz[...], R.wh[...])
+    step()
+    g2_grad, s2_grad = colsum(dm * R.m1[...]), colsum(dm)
+    rs2 = jnp.concatenate([R.rs2[...]] * 2, axis=1)
+    R.dh[...] = R.dh[...] + norm_back(dm * R.g2[...], R.m1[...], rs2)
+    step()
+    stat = tn(R.q[...], R.dh[...])
+    going = swap_start(3, compact(nt(stat, R.wo[...])))
+    step()
+    G[pl.ds(R_O, D)] = tn(R.KV[...], stat)
+    R.dq0[...] = turn_back(nt(R.dh[...], R.KVO[...]))
+    step()
+    G[pl.ds(R_Q, D)] = tn(R.n[...], R.dq0[...])
+    step()
+    launch(R_O, R_Q)
+    dkv = expand(swap_end(3, going))
+    G[pl.ds(R_V, D)] = tn(R.T[...], dkv)
+    step()
+    launch(R_V)
+    dt = nt(dkv, R.wv[...])
+    R.dk0[...] = turn_back(nt(R.wn[...], dt))
+    step()
+    G[pl.ds(R_K, D)] = tn(R.n[...], R.dk0[...])
+    step()
+    launch(R_K)
+    dn = (
+        nn(R.k[...], dt) * wgt2()
+        + nt(R.dq0[...], R.wq[...])
+        + nt(R.dk0[...], R.wk[...])
+    )
+    step()
+    g1_grad, s1_grad = colsum(dn * R.n1[...]), colsum(dn)
+    rs1 = jnp.concatenate([R.rs1[...]] * 2, axis=1)
+    R.dh[...] = R.dh[...] + norm_back(dn * R.g1[...], R.n1[...], rs1)
+    step()
+
+    cb_grad = colsum(R.dh[...])
+    conv_grad = nn(R.PT[...], R.dh[...])
+    small = [conv_grad[:, :128], conv_grad[:, 128:]]
+    vectors = [cb_grad, g1_grad, s1_grad, g2_grad, s2_grad, br_grad, ps_grad, bh_grad, bu_grad]
+    for v in vectors:
+        small += [v[:, 128 * k : 128 * (k + 1)] for k in range(v.shape[1] // 128)]
+    small.append(jnp.zeros((SMALL - sum(v.shape[0] for v in small), 128), f32))
+    small = jnp.concatenate(small, axis=0)
+    dpt = nt(R.W9[...], R.dh[...])
+    half_lane = iota((8, 2 * PTS), 1) // PTS == core
+    back = jnp.zeros((8, 2 * PTS), f32)
+    for di in range(3):
+        line = jnp.zeros((8, 2 * PTS), f32)
+        for dj in range(3):
+            part = dpt[(di * 3 + dj) * 8 : (di * 3 + dj) * 8 + 8]
+            part = jnp.where(half_lane, jnp.concatenate([part, part], axis=1), 0.0)
+            line = line + shift_cols(part, 1 - dj)
+        back = back + shift_rows(line, 1 - di)
+    back = jnp.where(full_mask, back, 0.0)
+    for k in range(DEVICES):
+        R.FS[pl.ds(16 * k, 8)] = small[8 * k : 8 * k + 8]
+        R.FS[pl.ds(16 * k + 8, 8)] = back[:, 128 * (k // 2) : 128 * (k // 2 + 1)]
+    step()
+    for k in range(1, DEVICES):
+        to = (me + k) % DEVICES
+        remote(
+            R.FS.at[pl.ds(to * 16, 12)],
+            R.FB.at[pl.ds(me * 16, 12)],
+            R.s_b.at[0],
+            R.r_b.at[0],
+            at(to),
+        )
+    R.FB[pl.ds(me * 16, 12)] = R.FS[pl.ds(me * 16, 12)]
+    step()
+
+    def small_sums():
+        drain(R.FB.at[pl.ds(0, 12 * (DEVICES - 1))], R.r_b.at[0])
+        total = jnp.zeros((8, 128), f32)
+        for k in range(DEVICES):
+            total = total + R.FB[pl.ds(16 * k, 8)]
+        mine = R.SS.at[pl.ds(me * 8, 8)]
+        mine[...] = total
+        for k in range(1, DEVICES):
+            remote(mine, mine, R.s_s.at[0], R.r_s.at[0], at((me + k) % DEVICES))
+        for b in range(ITEMS):
+            both = R.FB[pl.ds(32 * b + 8, 8)] + R.FB[pl.ds(32 * b + 24, 8)]
+            R.FO[pl.ds(8 * b, 8)] = jnp.where(core == 0, both, pltpu.roll(both, 64, 1))
+        out = pltpu.make_async_copy(R.FO, o_fg, R.s_o.at[len(CHUNKS) + 1])
+        out.start()
+        outs.append(out)
+
+    def small_end():
+        drain(R.SS.at[pl.ds(0, 8 * (DEVICES - 1))], R.r_s.at[0])
+        out = pltpu.make_async_copy(R.SS, o_small, R.s_o.at[len(CHUNKS) + 2])
+        out.start()
+        outs.append(out)
+
+    for i in TAIL:
+        if i == -1:
+            small_sums()
+        elif i == -2:
+            small_end()
+        else:
+            advance(i)
+    assert not going_on and not plan
+
+    drain(R.FR.at[pl.ds(0, 4 * (DEVICES - 1))], R.s_f.at[0])
+    drain(R.FB.at[pl.ds(0, 12 * (DEVICES - 1))], R.s_b.at[0])
+    drain(R.SS.at[pl.ds(0, 8 * (DEVICES - 1))], R.s_s.at[0])
+    inside_t = core == row // 2
+
+    @pl.when(inside_t)
+    def _():
+        drain(R.TS.at[pl.ds(0, 15)], R.s_t.at[0])
+        drain(R.DAB.at[pl.ds(0, 15)], R.s_r.at[0])
+
+    @pl.when(jnp.logical_not(inside_t))
+    def _():
+        drain(R.TS, R.s_t.at[0])
+        drain(R.DAB, R.s_r.at[0])
+
+    out_res.wait()
+    for out in outs:
+        out.wait()
+
+
+def vmem(*shape):
+    return pltpu.VMEM(shape, f32)
+
+
+SCRATCH = dict(
+    G=vmem(G_ROWS, D),
+    RB=vmem(G_ROWS, D),
+    SUM=vmem(G_ROWS, D),
+    FA=vmem(ITEMS * 8, 128),
+    FR=vmem(DEVICES * 8, 128),
+    FS=vmem(DEVICES * 16, 128),
+    FB=vmem(DEVICES * 16, 128),
+    FO=vmem(ITEMS * 8, 128),
+    SS=vmem(SMALL, 128),
+    W9=vmem(72, D),
+    XS=vmem(4, HEAD, D),
+    XR=vmem(4, HEAD, D),
+    TS=vmem(16, 16, D),
+    TR=vmem(ITEMS, 16, D),
+    DAB=vmem(ITEMS, 16, D),
+    DR=vmem(16, 16, D),
+    mask=vmem(PTS, 128),
+    wgt=vmem(PTS, 128),
+    ctm=vmem(PTS, D),
+    E=pltpu.VMEM((PTS, D), jnp.bfloat16),
+    dact=vmem(PTS, 512),
+    rcc=vmem(256, D),
+    rc=vmem(256, 512),
+    rot=vmem(PTS, D),
+    FF=vmem(96, 128),
+    PT=vmem(72, PTS),
+    h0=vmem(PTS, D),
+    rs1=vmem(PTS, 128),
+    n1=vmem(PTS, D),
+    n=vmem(PTS, D),
+    wn=vmem(PTS, D),
+    q=vmem(PTS, D),
+    k=vmem(PTS, D),
+    T=vmem(D, D),
+    KV=vmem(D, D),
+    KVO=vmem(D, D),
+    rs2=vmem(PTS, 128),
+    m1=vmem(PTS, D),
+    m=vmem(PTS, D),
+    h1=vmem(PTS, D),
+    a=vmem(PTS, 512),
+    az=vmem(PTS, 512),
+    h2=vmem(PTS, D),
+    gram=vmem(D, D),
+    DS=vmem(D, D),
+    P1=vmem(128, D),
+    AB=vmem(96, D),
+    UT=vmem(256, 512),
+    act=vmem(PTS, 512),
+    dpre=vmem(PTS, 512),
+    res=vmem(PTS, D),
+    dh=vmem(PTS, D),
+    dz=vmem(PTS, 512),
+    dq0=vmem(PTS, D),
+    dk0=vmem(PTS, D),
+    s_in=pltpu.SemaphoreType.DMA((len(INPUTS),)),
+    s_f=pltpu.SemaphoreType.DMA((1,)),
+    r_f=pltpu.SemaphoreType.DMA((1,)),
+    s_b=pltpu.SemaphoreType.DMA((1,)),
+    r_b=pltpu.SemaphoreType.DMA((1,)),
+    s_t=pltpu.SemaphoreType.DMA((1,)),
+    r_t=pltpu.SemaphoreType.DMA((16,)),
+    s_r=pltpu.SemaphoreType.DMA((1,)),
+    r_r=pltpu.SemaphoreType.DMA((16,)),
+    s_x=pltpu.SemaphoreType.DMA((4,)),
+    r_x=pltpu.SemaphoreType.DMA((4,)),
+    s_s=pltpu.SemaphoreType.DMA((1,)),
+    r_s=pltpu.SemaphoreType.DMA((1,)),
+    s_g=pltpu.SemaphoreType.DMA((SEMS * len(CHUNKS),)),
+    r_g=pltpu.SemaphoreType.DMA((SEMS * len(CHUNKS),)),
+    s_o=pltpu.SemaphoreType.DMA((3 + len(CHUNKS),)),
+)
+
+PARTS = dict(
+    wc=(9, 4, D),
+    cb=(1, D),
+    g1=(1, D),
+    s1=(1, D),
+    wq=(D, D),
+    wk=(D, D),
+    wv=(D, D),
+    wo=(D, D),
+    g2=(1, D),
+    s2=(1, D),
+    wh=(D, 512),
+    bh=(1, 512),
+    wr=(512, D),
+    br=(1, D),
+    dq=(128, D),
+    dk=(D, D),
+    dv=(D, D),
+    do=(D, D),
+    wu=(D, 512),
+    bu=(1, 512),
+    wd=(512, D),
+    ps=(1, D),
+)
+ROW_AT = dict(
+    wq=R_Q, wk=R_K, wv=R_V, wo=R_O, wr=R_RET, dq=R_DQ, dk=R_DK, dv=R_DV, do=R_DO, wd=R_DOWN,
+    wh=R_HID, wu=R_UP,
+)
+
+
+SMALL_PARTS = tuple(name for name in PARTS if name not in ROW_AT)
+
+
+def unpack(res_in, fg_in, small_in, g_in, res_out, fg_out, *rest):
+    outs = dict(zip(PARTS, rest[: len(PARTS)], strict=True))
+    res, fg, small, g, sem_in, sem_out, fg_here, *here = rest[len(PARTS) :]
+    staged = dict(zip(SMALL_PARTS, here, strict=True))
+    moves = []
+
+    def add(src, here, *out):
+        load = pltpu.make_async_copy(src, here, sem_in.at[len(moves)])
+        load.start()
+        moves.append((load, out))
+
+    add(small_in, small)
+    add(fg_in, fg)
+    for k in range(4):
+        part = pl.ds(k * 256, 256)
+        add(res_in.at[part], res.at[part], (res.at[part], res_out.at[part]))
+    for name, start in ROW_AT.items():
+        count = 512 if name in ("wh", "wu") else PARTS[name][0]
+        here = g.at[pl.ds(start, count)]
+        if name in ("wh", "wu"):
+            out = [
+                (g.at[pl.ds(start + s * D, D)], outs[name].at[:, pl.ds(s * D, D)])
+                for s in range(2)
+            ]
+        else:
+            out = [(here, outs[name])]
+        add(g_in.at[pl.ds(start, count)], here, *out)
+    stores = []
+
+    def store(src, dst):
+        stores.append(pltpu.make_async_copy(src, dst, sem_out.at[len(stores)]))
+        stores[-1].start()
+
+    moves[0][0].wait()
+    for k in range(9):
+        staged["wc"][k, :, :128] = small[S_CONV + 8 * k : S_CONV + 8 * k + 4]
+        staged["wc"][k, :, 128:] = small[S_CONV + 72 + 8 * k : S_CONV + 72 + 8 * k + 4]
+    line = S_VEC
+    for name in VECS:
+        for k in range(PARTS[name][1] // 128):
+            staged[name][:, 128 * k : 128 * (k + 1)] = small[line : line + 1]
+            line += 1
+    for name in SMALL_PARTS:
+        store(staged[name], outs[name])
+    moves[1][0].wait()
+    for ch in range(4):
+        fg_here[:, ch, :] = jnp.transpose(fg[pl.ds(ch, ITEMS, stride=8), pl.ds(0, 64)])
+    store(fg_here, fg_out)
+    for load, out in moves[2:]:
+        load.wait()
+        for src, dst in out:
+            store(src, dst)
+    for out in stores:
+        out.wait()
+
+
+ARGUMENTS = tuple(n for n in INPUTS if n not in ("fld", "ct"))
+
+
+def item_body(field_in, *rest):
+    values = dict(zip(ARGUMENTS + ("ct", "gs"), rest, strict=True))
+    values["fld"] = field_in.transpose(1, 2, 3, 0)
+    operands = [values["gs"].T]
+    operands += [values[name].reshape(shape) for name, shape in INPUTS.items()]
+    in_smem = pl.BlockSpec(memory_space=pltpu.SMEM)
+    anywhere = pl.BlockSpec(memory_space=pl.ANY)
+    made = pl.pallas_call(
+        kernel,
+        out_shape=(
+            jax.ShapeDtypeStruct((PTS, D), f32),
+            jax.ShapeDtypeStruct((ITEMS * 8, 128), f32),
+            jax.ShapeDtypeStruct((SMALL, 128), f32),
+            jax.ShapeDtypeStruct((G_ROWS, D), f32),
+        ),
+        in_specs=[in_smem] + [anywhere] * len(INPUTS),
+        out_specs=(anywhere,) * 4,
+        scratch_shapes=[*SCRATCH.values()] + [vmem(*shape) for shape in INPUTS.values()],
+        compiler_params=pltpu.CompilerParams(
+            collective_id=1, has_side_effects=True, vmem_limit_bytes=60 * 2**20
+        ),
+        name="layer",
+    )(*operands)
+    outs = pl.pallas_call(
+        unpack,
+        out_shape=(
+            jax.ShapeDtypeStruct((PTS, D), f32),
+            jax.ShapeDtypeStruct((NT * NT, 4, ITEMS), f32),
+            *(jax.ShapeDtypeStruct(shape, f32) for shape in PARTS.values()),
+        ),
+        in_specs=[anywhere] * 4,
+        out_specs=(anywhere,) * (2 + len(PARTS)),
+        scratch_shapes=[
+            vmem(PTS, D),
+            vmem(ITEMS * 8, 128),
+            vmem(SMALL, 128),
+            vmem(G_ROWS, D),
+            pltpu.SemaphoreType.DMA((24,)),
+            pltpu.SemaphoreType.DMA((40,)),
+            vmem(NT * NT, 4, ITEMS),
+            *(vmem(*PARTS[name]) for name in SMALL_PARTS),
+        ],
+        compiler_params=pltpu.CompilerParams(vmem_limit_bytes=60 * 2**20),
+        name="unpack",
+    )(*made)
+    shaped = []
+    for name, value in zip(PARTS, outs[2:], strict=True):
+        if name == "wc":
+            value = value.reshape(3, 3, 4, D)
+        elif name in VECS:
+            value = value.reshape(-1)
+        shaped.append(value)
     return (
-        result_field,
-        field_grad_all,
-        totals[0],
-        totals[1],
-        totals[2],
-        totals[3],
-        totals[4],
-        totals[5],
-        totals[6],
-        totals[7],
-        totals[8],
-        totals[9],
-        totals[10],
-        totals[11],
-        totals[12],
-        totals[13],
-        totals[14],
-        totals[15],
-        totals[16],
-        totals[17],
-        totals[18],
-        totals[19],
-        totals[20],
-        totals[21],
-    )
+        outs[0].reshape(ITEMS, NT, NT, D),
+        outs[1].reshape(NT, NT, 4, ITEMS).transpose(3, 0, 1, 2),
+        *shaped,
+    )
+
+
+def body(field_in, *rest):
+    tile = field_in.shape[:3]
+    mesh = (lax.axis_size("row"), lax.axis_size("col"))
+    if mesh == (ROWS, COLS) and tile == (ITEMS, NT, NT):
+        return item_body(field_in, *rest)
+    return general_body(field_in, *rest)
 
 
 def solution(mesh):
-    placed = (
-        P(None, "row", "col", None),
-        P(),
-        P(),
-        P(),
-        P(),
-        P(),
-        P(),
-        P(),
-        P(),
-        P(),
-        P(),
-        P(),
-        P(),
-        P(),
-        P(),
-        P(),
-        P(),
-        P(),
-        P(),
-        P(),
-        P(),
-        P(),
-        P(),
-        P(None, "row", "col", None),
-        P(),
-    )
+    spread = P(None, "row", "col", None)
+    placed = (spread,) + (P(),) * 22 + (spread, P())
     return jax.shard_map(
         body,
         mesh=mesh,
         in_specs=placed,
-        out_specs=(
-            P(None, "row", "col", None),
-            P(None, "row", "col", None),
-            P(),
-            P(),
-            P(),
-            P(),
-            P(),
-            P(),
-            P(),
-            P(),
-            P(),
-            P(),
-            P(),
-            P(),
-            P(),
-            P(),
-            P(),
-            P(),
-            P(),
-            P(),
-            P(),
-            P(),
-            P(),
-            P(),
-        ),
+        out_specs=(spread, spread) + (P(),) * 22,
         check_vma=False,
     )

time: 1420 us -> 110 us (0.08); the launches traced: 1400 us -> 110 us
  waiting for transfers between devices: 536 us -> 0 us
  matrix products: 410 us -> 0 us
  local copies, waits for them, and re-layouts: 233 us -> 0 us
  Pallas kernels: 0 us -> 109 us
  starting transfers between devices: 83.3 us -> 0 us
  other arithmetic: 78.2 us -> 0 us
  blocking collectives: 40.6 us -> 0 us
  between operations: 19.7 us -> 0.86 us
    psum x5 -> x0, waiting for transfers between devices: 524 us -> none  [the longest x1 132 us: body(): lax.psum(summary(key_heads, value_heads, weight), ('row', 'col'))]
    dot_general x272 -> x0, matrix products: 358 us -> none  [the longest x140 179 us: matmul(): return jnp.matmul(left, right, precision=highest)]
    pallas_call x0 -> x2, Pallas kernels: none -> 109 us  [the longest x1 104 us: item_body(): pl.pallas_call(kernel, out_shape=(jax.ShapeDtypeStruct((PTS, D), f32), ja...]
    reshape x64 -> x0, local copies, waits for them, and re-layouts: 108 us -> none  [the longest x48 77.9 us: split_heads(): return values.reshape(values.shape[:-1] + (HEADS, HEAD))]
    ppermute x32 -> x0, starting transfers between devices: 82.9 us -> none  [the longest x16 61.9 us: padded_2(): before = lax.ppermute(last, axis, up)]
    unnamed x1061 -> x0, local copies, waits for them, and re-layouts: 61.4 us -> none
    unnamed x24 -> x0, matrix products: 52.1 us -> none
    psum x1 -> x0, blocking collectives: 40.6 us -> none  [body(): lax.psum(tuple(encoder_total) + tuple(decoder_total), ('row', 'col'))]
  transfers between devices with their start and end apart: 37 -> 0, of which waited for: 10 -> 0; matrix products, arithmetic and copies ran while one was open for 8% -> 0% of each run, Pallas kernels for 0% -> 0%
where the time goes in v1:
time: 110 us
  Pallas kernels  109 us (99%)
    pallas_call x1, Pallas kernels, item_body(): pl.pallas_call(kernel, out_shape=(jax.ShapeDtypeStruct((PTS, D), f32), ja...  104 us
    pallas_call x1, Pallas kernels, item_body(): pl.pallas_call(unpack, out_shape=(jax.ShapeDtypeStruct((PTS, D), f32), ja...  5.32 us

profile of v1, /device:TPU:0, one launch (start us, length us, event | category | flops | bytes accessed | tf_op | source)
XLA Modules:
  0.0 110.3 jit_solution(13809594683235245194)
XLA Ops:
  0.7 104.1 %layer.1 = (f32[1024,256]{1,0:T(8,128)}, f32[128,128]{1,0:T(8,128)}, f32[256,128]{1,0:T(8,128)}, f32[4096,256]{1,0:T(8,128)}) custom-call(s32[2,16]{1,0:T(2,128)} %bitcast.34, f32[64,4,16]{2,1,0:T(4,128)} %bitcast.30, f32[1024,256]{1,0:T(8,128)} %bitcast.29, f32[9,4,256]{2,1,0:T(4,128)} %bitcast.31, f32[1,256]{1,0:T(1,128)} %bitcast.35, f32[1,256]{1,0:T(1,128)} %bitcast.36, ...), custom_call_target="tpu_custom_call" | custom-call | tf_op jit(solution)/shard_map/layer/pallas_call | solution.py:1202
  104.8 5.3 %unpack.1 = (f32[1024,256]{1,0:T(8,128)}, f32[64,4,16]{2,1,0:T(4,128)}, f32[9,4,256]{2,1,0:T(4,128)}, f32[1,256]{1,0:T(1,128)}, f32[1,256]{1,0:T(1,128)}, /*inde...) custom-call(f32[1024,256]{1,0:T(8,128)} %get-tuple-element.52.res_in, ...), custom_call_target="tpu_custom_call" | custom-call | tf_op jit(solution)/shard_map/unpack/pallas_call | solution.py:1218
